TPU v7x, 512 devices: a whole 4x8x8 slice. The times are simulated.
512 devices in a mesh: req: 32 (over z, x), tp: 16 (over y, core).
Axes of the slice: x: 4, y: 8, z: 8, core: 2. Of those that a mesh axis runs over, the one named last changes fastest.
Arguments:
- passage_cache: bfloat16 [256, 512, 2048], P('req', None, 'tp'), may hold values from -6 to 6
- kv_weight: bfloat16 [8192, 2048], P(None, 'tp'), may hold values from -0.0625 to 0.0625
- block_hidden: bfloat16 [32, 256, 8192], P('req', None, 'tp'), may hold values from -6 to 6
- new_hidden: bfloat16 [32, 512, 8192], P('req', None, 'tp'), may hold values from -6 to 6
- queries: bfloat16 [32, 512, 8192], P('req', None, 'tp'), may hold values from -100 to 100
- passage_ids: int32 [32, 8], replicated, may hold values from 0 to 255, as said below
- passage_starts: int32 [32, 9], P('req'), may hold values from 0 to 4855, as said below
- recompute_blocks: int32 [32, 2], P('req'), may hold values from 0 to 31, as said below
- passage_counts: int32 [32], P('req'), may hold values from 1 to 8
Outputs:
- attended: bfloat16 [32, 512, 8192], P('req', None, 'tp')
Inputs may be any that keep to these rules, and one draw needn't show every extreme that they name: `passage_ids`: A request's 8 entries are distinct; row i is stored on req index i // 8; no request takes more than 1 row from one req index. `passage_starts`: each row rises; its first entry is at most 255, and consecutive entries lie 512 to 575 apart. `recompute_blocks`: distinct within a request.
All inputs are finite; a program needn't handle non-finite values.
Results may differ from a plain program's by a relative error of at most 0.024.
Values may be sent and summed in bfloat16 or wider, within the bound.
No kernel may reach another device: no remote copies, remote signals or barrier semaphores. Data moves between devices by JAX's collectives and lax.ppermute only.
A program may use at most 128 MiB of HBM per device.

v0:
```python
import jax
import jax.numpy as jnp
from jax import lax
from jax.sharding import PartitionSpec as P

HD = 128


THETA = 500000.0


def from_partner(block, axis, apart):
    count = lax.axis_size(axis)
    route = []
    for low in range(count):
        high = low | 1 << apart
        if high != low and high < count:
            route += [(low, high), (high, low)]
    return lax.ppermute(block, axis, route)


def rotate(values, positions):
    half = HD // 2
    rates = THETA ** (-(jnp.arange(half, dtype=jnp.float32) * 2.0 / HD))
    angle = positions[:, None] * rates[None, :]
    cosine = jnp.cos(angle)[:, None, :]
    sine_part = jnp.sin(angle)[:, None, :]
    per_head = values.reshape(values.shape[0], -1, HD)
    first = per_head[:, :, :half]
    second = per_head[:, :, half:]
    turned = jnp.concatenate(
        [first * cosine - second * sine_part, second * cosine + first * sine_part], axis=2
    )
    return turned.reshape(values.shape[0], -1)


def score_block(query_part, key_part):
    return lax.dot_general(
        query_part, key_part, (((1,), (1,)), ((), ())), preferred_element_type=jnp.float32
    ) * HD ** (-0.5)


def attend(query_part, key_part, value_part, allowed):
    scores = score_block(query_part, key_part)
    scores = jnp.where(allowed, scores, -1e30)
    top_score = jnp.max(scores, axis=1, keepdims=True)
    weights = jnp.exp(scores - top_score)
    weights = (weights / jnp.sum(weights, axis=1, keepdims=True)).astype(jnp.bfloat16)
    return jnp.dot(weights, value_part, preferred_element_type=jnp.float32).astype(jnp.bfloat16)


def body(
    passage_cache,
    kv_weight,
    block_hidden,
    new_hidden,
    queries,
    passage_ids,
    passage_starts,
    recompute_blocks,
    passage_counts,
):
    req_total = lax.axis_size("req")
    tp_total = lax.axis_size("tp")
    req_index = lax.axis_index("req")
    tp_index = lax.axis_index("tp")
    store_dev = passage_cache.shape[0]
    length = passage_cache.shape[1]
    local_cols = passage_cache.shape[2]
    passages = passage_ids.shape[1]
    capacity = (passages + req_total - 1) // req_total
    owners = passage_ids // store_dev
    slots = passage_ids % store_dev
    earlier = jnp.arange(passages)[:, None] > jnp.arange(passages)[None, :]
    same_owner = owners[:, :, None] == owners[:, None, :]
    ranks = jnp.sum(jnp.logical_and(same_owner, earlier[None]), axis=2)
    picks = jnp.logical_and(
        (owners == req_index)[:, None, :],
        ranks[:, None, :] == jnp.arange(capacity, dtype=jnp.int32)[None, :, None],
    )
    local_rows = jnp.sum(jnp.where(picks, slots[:, None, :], 0), axis=2)
    outgoing = jnp.take(passage_cache, local_rows.reshape(-1), axis=0).reshape(
        req_total, capacity, length, local_cols
    )
    incoming = lax.all_to_all(outgoing, "req", split_axis=0, concat_axis=0, tiled=True)
    mine_owner = lax.dynamic_index_in_dim(owners, req_index, 0, keepdims=False)
    mine_rank = lax.dynamic_index_in_dim(ranks, req_index, 0, keepdims=False)
    flat_index = mine_owner * capacity + mine_rank
    fetched = jnp.take(
        incoming.reshape(req_total * capacity, length, local_cols), flat_index, axis=0
    ).reshape(passages * length, local_cols)
    starts = passage_starts[0]
    is_key = tp_index < tp_total // 2
    passage_of = jnp.arange(passages * length, dtype=jnp.int32) // length
    shifted = rotate(fetched.astype(jnp.float32), starts[passage_of].astype(jnp.float32))
    context_rows = jnp.where(is_key, shifted.astype(jnp.bfloat16), fetched)
    block_rows = block_hidden.shape[1]
    new_count = new_hidden.shape[1]
    local_stack = jnp.concatenate([block_hidden[0], new_hidden[0]], axis=0)
    projected = jnp.dot(
        lax.all_gather(local_stack, "tp", axis=1, tiled=True),
        kv_weight,
        preferred_element_type=jnp.float32,
    )
    blocks = recompute_blocks[0]
    block_size = block_rows // blocks.shape[0]
    within = jnp.arange(block_rows, dtype=jnp.int32)
    context_index = blocks[within // block_size] * block_size + within % block_size
    block_positions = starts[context_index // length] + context_index % length
    new_positions = starts[passages] + jnp.arange(new_count, dtype=jnp.int32)
    positions = jnp.concatenate([block_positions, new_positions]).astype(jnp.float32)
    turned = rotate(projected, positions)
    fresh = jnp.where(is_key, turned, projected).astype(jnp.bfloat16)
    updated = context_rows
    for number in range(blocks.shape[0]):
        updated = lax.dynamic_update_slice_in_dim(
            updated,
            fresh[number * block_size : (number + 1) * block_size],
            blocks[number] * block_size,
            0,
        )
    own_rows = jnp.concatenate([updated, fresh[block_rows:]], axis=0)
    partner_rows = from_partner(own_rows, "tp", tp_total.bit_length() - 2)
    all_keys = jnp.where(is_key, own_rows, partner_rows)
    all_values = jnp.where(is_key, partner_rows, own_rows)
    context_len = passages * length
    rows_new = jnp.arange(new_count, dtype=jnp.int32)
    query_rows = queries[0]
    local_heads = query_rows.shape[1] // HD
    live_count = passage_counts[0]
    columns = jnp.arange(context_len + new_count, dtype=jnp.int32)
    in_context = columns < context_len
    allowed = jnp.where(
        in_context[None, :],
        (columns // length)[None, :] < live_count,
        (columns - context_len)[None, :] <= rows_new[:, None],
    )

    def one_head(head):
        query_part = lax.dynamic_slice_in_dim(query_rows, head * HD, HD, 1)
        return attend(query_part, all_keys, all_values, allowed)

    outputs = lax.map(one_head, jnp.arange(local_heads, dtype=jnp.int32))
    return jnp.transpose(outputs, (1, 0, 2)).reshape(1, new_count, local_heads * HD)


def solution(mesh):
    in_specs = (
        P("req", None, "tp"),
        P(None, "tp"),
        P("req", None, "tp"),
        P("req", None, "tp"),
        P("req", None, "tp"),
        P(),
        P("req", None),
        P("req", None),
        P("req"),
    )
    out_specs = P("req", None, "tp")
    return jax.shard_map(body, mesh=mesh, in_specs=in_specs, out_specs=out_specs, check_vma=False)
```

profile of v0, /device:TPU:38, one launch (start us, length us, event | category | flops | bytes accessed | tf_op | source)
XLA Modules:
  0.0 263.1 jit_solution(15173040247640593180)
XLA Ops:
  6.5 2.2 pad_maximum_fusion.1
  9.0 3.0 %gather_fusion = bf16[32,512,128]{2,1,0:T(8,128)(2,1)} fusion(bf16[8,512,128]{2,1,0:T(8,128)(2,1)S(1)} %copy-done.1, s32[1024]{0:T(1024)S(1)} %pad_clamp_fusion.1), kind=kCustom, calls=%fused_computation | custom fusion | bytes 8388736 | tf_op jit(solution)/shard_map/jit(_take)/gather | solution.py:82
  12.0 4.6 %bitcast_select_fusion = bf16[32,1,512,128]{3,2,1,0:T(8,128)(2,1)} fusion(bf16[32,512,128]{2,1,0:T(8,128)(2,1)} %gather_fusion, pred[32]{0:T(512)(128)(4,1)S(1)} %compare_and_fusion), kind=kLoop, calls=%fused_computation.15 | loop fusion | flops 2097152 | bytes 8388640 | tf_op jit(solution)/shard_map/jit(_take)/select_n | solution.py:82
  16.6 13.6 %all-to-all-start = ((bf16[32,1,512,128]{3,2,1,0:T(8,128)(2,1)}), bf16[32,1,512,128]{3,2,1,0:T(8,128)(2,1)}, u32[]{:S(2)}, u32[]{:S(2)}) async-start(bf16[32,1,512,128]{3,2,1,0:T(8,128)(2,1)} %bitcast_select_fusion), calls=%async_computation | async-start | bytes 8388608 | tf_op jit(solution)/shard_map/all_to_all | solution.py:85
  35.1 5.5 %compare_select_fusion.9 = (s32[256,1]{0,1:T(1,128)S(1)}, s32[256,1]{0,1:T(1,128)S(1)}) fusion(s32[]{:T(128)} %bitcast.9, s32[]{:T(128)} %bitcast.10, s32[]{:T(128)} %bitcast.11, s32[]{:T(128)} %bitcast.12, s32[]{:T(128)} %bitcast.13, s32[]{:T(128)} %bitcast.15, s32[]{:T(128)} %bitcast.14, s32[]{:T(128)} %bitcast.23, s32[]{:T(128)} %bitcast.22), kind=kLoop, calls=%fused_computation.90 | loop fusion | flops 12544 | bytes 2084 | tf_op jit(solution)/shard_map/gather | solution.py:109
  41.9 4.2 %compare_select_fusion.1 = s32[4096,1]{0,1:T(1,128)S(1)} fusion(s32[]{:T(128)} %bitcast.9, s32[]{:T(128)} %bitcast.10, s32[]{:T(128)} %bitcast.11, s32[]{:T(128)} %bitcast.12, s32[]{:T(128)} %bitcast.13, s32[]{:T(128)} %bitcast.15, s32[]{:T(128)} %bitcast.14), kind=kLoop, calls=%fused_computation.47 | loop fusion | flops 94208 | bytes 16412 | tf_op jit(solution)/shard_map/gather | solution.py:95
  47.5 78.4 %all-to-all-done = bf16[32,1,512,128]{3,2,1,0:T(8,128)(2,1)} async-done(((bf16[32,1,512,128]{3,2,1,0:T(8,128)(2,1)}), bf16[32,1,512,128]{3,2,1,0:T(8,128)(2,1)}, u32[]{:S(2)}, u32[]{:S(2)}) %all-to-all-start) | async-done | bytes 4194336 | tf_op jit(solution)/shard_map/all_to_all | solution.py:85
  125.9 2.9 %gather_fusion.1 = bf16[8,512,128]{2,1,0:T(8,128)(2,1)S(1)} fusion(bf16[32,512,128]{2,1,0:T(8,128)(2,1)} %bitcast.4, s32[1024]{0:T(1024)S(1)} %pad_clamp_fusion), kind=kCustom, calls=%fused_computation.1 | custom fusion | bytes 2097184 | tf_op jit(solution)/shard_map/jit(_take)/gather | solution.py:89
  132.9 4.2 %fusion.15 = (bf16[4096,1,64]{0,2,1:T(8,128)(2,1)S(1)}, bf16[4096,1,64]{0,2,1:T(8,128)(2,1)S(1)}) fusion(f32[4096,1,128]{0,2,1:T(8,128)S(1)} %select_convert_fusion, f32[64]{0:T(128)S(1)} %negate_power_fusion, f32[4096]{0:T(1024)S(1)} %select_convert_fusion.1), kind=kLoop, calls=%fused_computation.26 | loop fusion | flops 2359296 | bytes 3162368 | tf_op jit(solution)/shard_map/convert
  137.5 8.9 %fusion.45 = f32[768,128]{0,1:T(8,128)S(1)} fusion(bf16[768,8192]{1,0:T(8,128)(2,1)} %all-gather.2.cloned.1.call-done, bf16[8192,128]{1,0:T(8,128)(2,1)S(1)} %copy-done), kind=kOutput, calls=%fused_computation.129 | convolution fusion | flops 1610612736 | bytes 15073280 | tf_op jit(solution)/shard_map/dot_general | solution.py:100
  148.4 2.2 collective-permute-start
  151.3 56.6 %collective-permute-done = bf16[4608,128]{0,1:T(8,128)(2,1)} collective-permute-done((bf16[4608,128]{0,1:T(8,128)(2,1)}, bf16[4608,128]{0,1:T(8,128)(2,1)}, u32[]{:S(2)}, u32[]{:S(2)}) %collective-permute-start) | collective-permute-done | bytes 1179680 | tf_op jit(solution)/shard_map/ppermute | solution.py:19
  208.0 3.1 %broadcast_select_fusion = (bf16[4608,128]{0,1:T(8,128)(2,1)}, bf16[4608,128]{0,1:T(8,128)(2,1)}) fusion(bf16[4608,128]{0,1:T(8,128)(2,1)} %collective-permute-done, pred[]{:T(512)S(6)} %lt.123, bf16[512,128]{0,1:T(8,128)(2,1)S(1)} %slice.99, bf16[4096,128]{0,1:T(8,128)(2,1)S(1)} %slice_dynamic-update-slice_fusion), kind=kLoop, calls=%fused_computation.23 | loop fusion | flops 3538944 | bytes 4718593 | tf_op jit(solution)/shard_map/jit(_where)/select_n | solution.py:125
  211.0 2.5 copy.38
  214.9 38.9 %while.11 = (s32[]{:T(128)}, bf16[4,512,128]{2,1,0:T(8,128)(2,1)}, s32[4]{0:T(128)S(1)}, bf16[512,512]{1,0:T(8,128)(2,1)}, bf16[4608,128]{1,0:T(8,128)(2,1)}, /*...) while((s32[]{:T(128)}, bf16[4,512,128]{2,1,0:T(8,128)(2,1)}, ...), condition=%wide.region_5.6_spmd.clone, body=%wide.region_2.5_spmd.clone.sunk | while | flops 1231617024 | bytes 35689696 | solution.py:143
  216.0 4.3 %fusion.57 = (f32[512]{0:T(512)S(1)}, f32[512,4608]{1,0:T(8,128)S(1)}) fusion(bf16[4608,128]{1,0:T(8,128)(2,1)} %get-tuple-element.207, bf16[512,512]{1,0:T(8,128)(2,1)} %get-tuple-element.206, s32[]{:T(128)S(6)} %select_n.382, s32[4608]{0:T(1024)S(1)} %get-tuple-element.209, pred[4608]{0:T(1024)(128)(4,1)S(1)} %get-tuple-element.210, ...), kind=kOutput, calls=%fused_computation.126.clone.1 | convolution fusion | flops 615775744 | bytes 10777604 | tf_op jit(solution)/shard_map/while/body/eval_jaxpr/dot_general | solution.py:38
  221.8 2.8 %fusion.59 = bf16[4,512,128]{2,1,0:T(8,128)(2,1)} fusion(bf16[4,512,128]{2,1,0:T(8,128)(2,1)} %get-tuple-element.191, s32[]{:T(128)S(6)} %copy.49, bf16[4608,128]{1,0:T(8,128)(2,1)S(1)} %copy-done.4, f32[512,4608]{1,0:T(8,128)S(1)} %get-tuple-element.175, f32[512]{0:T(512)S(1)} %fusion.58, f32[512]{0:T(512)S(1)} %get-tuple-element.176), kind=kOutput, calls=%fused_computation.12.clone.1 | convolution fusion | flops 611123200 | bytes 10752004 | tf_op jit(solution)/shard_map/while/body/eval_jaxpr/dot_general | solution.py:49
  225.8 4.3 %fusion.57 = (f32[512]{0:T(512)S(1)}, f32[512,4608]{1,0:T(8,128)S(1)}) fusion(bf16[4608,128]{1,0:T(8,128)(2,1)} %get-tuple-element.207, bf16[512,512]{1,0:T(8,128)(2,1)} %get-tuple-element.206, s32[]{:T(128)S(6)} %select_n.382, s32[4608]{0:T(1024)S(1)} %get-tuple-element.209, pred[4608]{0:T(1024)(128)(4,1)S(1)} %get-tuple-element.210, ...), kind=kOutput, calls=%fused_computation.126.clone.1 | convolution fusion | flops 615775744 | bytes 10777604 | tf_op jit(solution)/shard_map/while/body/eval_jaxpr/dot_general | solution.py:38
  231.5 2.8 %fusion.59 = bf16[4,512,128]{2,1,0:T(8,128)(2,1)} fusion(bf16[4,512,128]{2,1,0:T(8,128)(2,1)} %get-tuple-element.191, s32[]{:T(128)S(6)} %copy.49, bf16[4608,128]{1,0:T(8,128)(2,1)S(1)} %copy-done.4, f32[512,4608]{1,0:T(8,128)S(1)} %get-tuple-element.175, f32[512]{0:T(512)S(1)} %fusion.58, f32[512]{0:T(512)S(1)} %get-tuple-element.176), kind=kOutput, calls=%fused_computation.12.clone.1 | convolution fusion | flops 611123200 | bytes 10752004 | tf_op jit(solution)/shard_map/while/body/eval_jaxpr/dot_general | solution.py:49
  235.5 4.3 %fusion.57 = (f32[512]{0:T(512)S(1)}, f32[512,4608]{1,0:T(8,128)S(1)}) fusion(bf16[4608,128]{1,0:T(8,128)(2,1)} %get-tuple-element.207, bf16[512,512]{1,0:T(8,128)(2,1)} %get-tuple-element.206, s32[]{:T(128)S(6)} %select_n.382, s32[4608]{0:T(1024)S(1)} %get-tuple-element.209, pred[4608]{0:T(1024)(128)(4,1)S(1)} %get-tuple-element.210, ...), kind=kOutput, calls=%fused_computation.126.clone.1 | convolution fusion | flops 615775744 | bytes 10777604 | tf_op jit(solution)/shard_map/while/body/eval_jaxpr/dot_general | solution.py:38
  241.2 2.8 %fusion.59 = bf16[4,512,128]{2,1,0:T(8,128)(2,1)} fusion(bf16[4,512,128]{2,1,0:T(8,128)(2,1)} %get-tuple-element.191, s32[]{:T(128)S(6)} %copy.49, bf16[4608,128]{1,0:T(8,128)(2,1)S(1)} %copy-done.4, f32[512,4608]{1,0:T(8,128)S(1)} %get-tuple-element.175, f32[512]{0:T(512)S(1)} %fusion.58, f32[512]{0:T(512)S(1)} %get-tuple-element.176), kind=kOutput, calls=%fused_computation.12.clone.1 | convolution fusion | flops 611123200 | bytes 10752004 | tf_op jit(solution)/shard_map/while/body/eval_jaxpr/dot_general | solution.py:49
  245.2 4.3 %fusion.57 = (f32[512]{0:T(512)S(1)}, f32[512,4608]{1,0:T(8,128)S(1)}) fusion(bf16[4608,128]{1,0:T(8,128)(2,1)} %get-tuple-element.207, bf16[512,512]{1,0:T(8,128)(2,1)} %get-tuple-element.206, s32[]{:T(128)S(6)} %select_n.382, s32[4608]{0:T(1024)S(1)} %get-tuple-element.209, pred[4608]{0:T(1024)(128)(4,1)S(1)} %get-tuple-element.210, ...), kind=kOutput, calls=%fused_computation.126.clone.1 | convolution fusion | flops 615775744 | bytes 10777604 | tf_op jit(solution)/shard_map/while/body/eval_jaxpr/dot_general | solution.py:38
  251.0 2.8 %fusion.59 = bf16[4,512,128]{2,1,0:T(8,128)(2,1)} fusion(bf16[4,512,128]{2,1,0:T(8,128)(2,1)} %get-tuple-element.191, s32[]{:T(128)S(6)} %copy.49, bf16[4608,128]{1,0:T(8,128)(2,1)S(1)} %copy-done.4, f32[512,4608]{1,0:T(8,128)S(1)} %get-tuple-element.175, f32[512]{0:T(512)S(1)} %fusion.58, f32[512]{0:T(512)S(1)} %get-tuple-element.176), kind=kOutput, calls=%fused_computation.12.clone.1 | convolution fusion | flops 611123200 | bytes 10752004 | tf_op jit(solution)/shard_map/while/body/eval_jaxpr/dot_general | solution.py:49
  253.8 1.4 copy.40
  (72 shorter events, 23.2 us)
Async XLA Ops:
  6.5 131.0 %copy-start = (bf16[8192,128]{1,0:T(8,128)(2,1)S(1)}, bf16[8192,128]{1,0:T(8,128)(2,1)}, u32[]{:S(2)}) copy-start(bf16[8192,128]{1,0:T(8,128)(2,1)} %param.12) | copy-start | bytes 6291460
  6.5 2.2 copy-start.6
  6.5 2.4 copy-start.1
  6.5 130.9 %all-gather.2.cloned.1.call-start = ((), (), s32[]{:S(2)}) async-start(), calls=%async_computation.1 | async-start | bytes 13369344 | tf_op jit(solution)/shard_map/all_gather | solution.py:101
  16.6 13.6 %copy-start.7 = (s32[1,2]{1,0:T(1,128)S(1)}, s32[1,2]{1,0:T(1,128)}, u32[]{:S(2)}) copy-start(s32[1,2]{1,0:T(1,128)} %param.18) | copy-start | bytes 28
  16.6 17.2 %copy-start.5 = (s32[1,9]{1,0:T(1,128)S(1)}, s32[1,9]{1,0:T(1,128)}, u32[]{:S(2)}) copy-start(s32[1,9]{1,0:T(1,128)} %param.17) | copy-start | bytes 112
  16.6 109.3 %all-to-all-start = ((bf16[32,1,512,128]{3,2,1,0:T(8,128)(2,1)}), bf16[32,1,512,128]{3,2,1,0:T(8,128)(2,1)}, u32[]{:S(2)}, u32[]{:S(2)}) async-start(bf16[32,1,512,128]{3,2,1,0:T(8,128)(2,1)} %bitcast_select_fusion), calls=%async_computation | async-start | bytes 8388608 | tf_op jit(solution)/shard_map/all_to_all | solution.py:85
  132.9 4.2 %copy-start.3 = (bf16[4096,128]{0,1:T(8,128)(2,1)S(1)}, bf16[4096,128]{0,1:T(8,128)(2,1)}, u32[]{:S(2)}) copy-start(bf16[4096,128]{0,1:T(8,128)(2,1)} %copy.42) | copy-start | bytes 3145732
  148.4 59.5 %collective-permute-start = (bf16[4608,128]{0,1:T(8,128)(2,1)}, bf16[4608,128]{0,1:T(8,128)(2,1)}, u32[]{:S(2)}, u32[]{:S(2)}) collective-permute-start(bf16[4608,128]{0,1:T(8,128)(2,1)} %pad_maximum_fusion), channel_id=1, source_target_pairs={{0,8},{8,0},{1,9},{9,1},{2,10},{10,2},{3,11},{11,3},{4,12},{12,4},... | collective-permute-start | bytes 3538952 | tf_op jit(solution)/shard_map/ppermute | solution.py:19
  211.0 2.5 copy-start.2
  220.4 1.4 copy-start.4
  230.1 1.4 copy-start.4
  239.8 1.4 copy-start.4
  249.5 1.4 copy-start.4
Sparse Core Ops, SparseCore 0:
  9.5 79.8 all-gather.1
where the time goes:
time: 264 us; the launch traced here: 263 us
  waiting for transfers between devices  135 us (51%)
  other arithmetic  38 us (14%)
  matrix products  37.5 us (14%)
  local copies, waits for them, and re-layouts  18.7 us (7%)
  starting transfers between devices  15.8 us (6%)
  between operations  15.6 us (6%)
    all_to_all x1, waiting for transfers between devices, body(): lax.all_to_all(outgoing, 'req', split_axis=0, concat_axis=0, tiled=True)  78.4 us
    ppermute x1, waiting for transfers between devices, from_partner(): return lax.ppermute(block, axis, route)  56.6 us
    dot_general x4, matrix products, score_block(): lax.dot_general(query_part, key_part, (((1,), (1,)), ((), ())), preferred...  17.3 us
    all_to_all x1, starting transfers between devices, body(): lax.all_to_all(outgoing, 'req', split_axis=0, concat_axis=0, tiled=True)  13.6 us
    dot_general x4, matrix products, attend(): jnp.dot(weights, value_part, preferred_element_type=jnp.float32)  11.4 us
    dot_general x1, matrix products, body(): jnp.dot(lax.all_gather(local_stack, 'tp', axis=1, tiled=True), kv_weight,...  8.86 us
    gather x2, other arithmetic, body(): block_positions = starts[context_index // length] + context_index % length  6.76 us
    reduce_sum x4, other arithmetic, attend(): jnp.sum(weights, axis=1, keepdims=True)  5.61 us
  transfers between devices with their start and end apart: 3, of which 2 were waited for; matrix products, arithmetic and copies ran while one was open for 13% of the time, Pallas kernels for 0%

commit v1 on v0

v1 whole, which is shorter than its diff:
```python
import functools

import jax
import jax.numpy as jnp
from jax import lax
from jax.experimental import pallas as pl
from jax.experimental.pallas import tpu as pltpu
from jax.sharding import PartitionSpec as P

HD = 128
THETA = 500000.0
LOG2E = 1.4426950408889634
SCALE = HD ** (-0.5) * LOG2E
NEG = -1e30
QT = 256
KC = 512
BLK = 128
F32 = jnp.float32
BF16 = jnp.bfloat16
GROUPS = ((0, 4), (4, 8))


def tables(positions):
    rates = THETA ** (-(jnp.arange(HD // 2, dtype=F32) * 2.0 / HD))
    angle = positions.astype(F32)[:, None] * rates[None, :]
    cosine, sine = jnp.cos(angle), jnp.sin(angle)
    return jnp.concatenate([cosine, cosine], axis=1), jnp.concatenate([-sine, sine], axis=1)


def turn(values, cosine, sine):
    half = HD // 2
    swapped = jnp.concatenate([values[:, half:], values[:, :half]], axis=1)
    return values * cosine + swapped * sine


def partner(block, tp_total):
    half = tp_total // 2
    return lax.ppermute(block, "tp", [(i, (i + half) % tp_total) for i in range(tp_total)])


def pick_kernel(count, ids, pieces, out):
    def step(i, _):
        out[i] = pieces[ids[i]]
        return 0

    lax.fori_loop(0, count, step, 0, unroll=16)


def pick(pieces, ids):
    count = ids.shape[0]
    return pl.pallas_call(
        functools.partial(pick_kernel, count),
        out_shape=jax.ShapeDtypeStruct((count,) + pieces.shape[1:], pieces.dtype),
        in_specs=[pl.BlockSpec(memory_space=pltpu.SMEM), pl.BlockSpec(memory_space=pltpu.VMEM)],
        out_specs=pl.BlockSpec(memory_space=pltpu.VMEM),
        compiler_params=pltpu.CompilerParams(vmem_limit_bytes=16 * 2**20),
        cost_estimate=pl.CostEstimate(flops=0, bytes_accessed=count * 8192, transcendentals=0),
        name="pick",
    )(ids, pieces)


def scores_into(store, keys, kx, weights, causal_from, column):
    top = None
    for c in range(0, keys, BLK * 2):
        part = jnp.dot(kx[c : c + BLK * 2, :], weights, preferred_element_type=F32)
        if causal_from is not None and c >= causal_from:
            row = lax.broadcasted_iota(jnp.int32, part.shape, 0) + (c - causal_from)
            query = lax.broadcasted_iota(jnp.int32, part.shape, 1) + column
            part = jnp.where(row <= query, part, NEG)
        store[c : c + BLK * 2, :] = part
        high = jnp.max(part.reshape(BLK * 2 // 8, 8, part.shape[1]), axis=0)
        top = high if top is None else jnp.maximum(top, high)
    return jnp.max(top, axis=0, keepdims=True) * SCALE


def weigh(store, keys, vt, top):
    total = None
    for c in range(0, keys, BLK * 2):
        weights = jnp.exp2(store[c : c + BLK * 2, :] * SCALE - top).astype(BF16)
        part = jnp.dot(vt[:, c : c + BLK * 2], weights, preferred_element_type=F32)
        total = part if total is None else total + part
    return total


def fill_queries(q_ref, qx, heads, rows):
    for h in range(heads):
        qx[0:HD, h * rows : (h + 1) * rows] = q_ref[:, h * HD : (h + 1) * HD].T
    first = lax.broadcasted_iota(jnp.int32, (HD, heads * rows), 0) == 0
    qx[HD:, :] = jnp.where(first, 1.0, 0.0).astype(BF16)


def bias_block(value):
    lane = lax.broadcasted_iota(jnp.int32, (BLK, HD), 1)
    return jnp.where(lane == 0, value, 0.0).astype(BF16)


def run_tiles(tiles, keys, kx, vt, qx, sa, sb, rows, causal_from, put):
    def weights_of(i):
        return qx[:, pl.ds(pl.multiple_of(i * QT, QT), QT)]

    def column_of(i):
        return lax.rem(i * QT, rows)

    top = scores_into(sa, keys, kx, weights_of(0), causal_from, 0)

    def step(j, top_a):
        i = 2 * j
        top_b = scores_into(sb, keys, kx, weights_of(i + 1), causal_from, column_of(i + 1))
        put(i, top_a, weigh(sa, keys, vt, top_a))
        later = jnp.minimum(i + 2, tiles - 1)
        top_a = scores_into(sa, keys, kx, weights_of(later), causal_from, column_of(later))
        put(i + 1, top_b, weigh(sb, keys, vt, top_b))
        return top_a

    lax.fori_loop(0, tiles // 2, step, top)


def context_kernel(low, high, sizes, scalars, q_ref, cos_ref, sin_ref, own, other, total, tops, qx, kx, vt, sa, sb):
    heads, rows, length = sizes
    keys = (high - low) * length
    is_key = scalars[0] == 1
    fill_queries(q_ref, qx, heads, rows)
    vt[HD:, :] = jnp.ones((16, keys), BF16)
    for s in range(high - low):
        mine = own[:, s].reshape(length, HD)
        theirs = other[:, s].reshape(length, HD)
        raw = jnp.where(is_key, mine, theirs).astype(F32)
        cosine = cos_ref[low + s : low + s + 1, :]
        sine = sin_ref[low + s : low + s + 1, :]
        base = s * length
        kx[base : base + length, :HD] = (raw * cosine + pltpu.roll(raw, HD // 2, 1) * sine).astype(BF16)
        vt[:HD, base : base + length] = jnp.where(is_key, theirs, mine).T
        for b in range(length // BLK):
            number = (low + s) * (length // BLK) + b
            hidden = jnp.logical_or(number == scalars[2], number == scalars[3])
            hidden = jnp.logical_or(hidden, low + s >= scalars[1])
            kx[base + b * BLK : base + (b + 1) * BLK, HD:] = bias_block(jnp.where(hidden, NEG, 0.0))

    def put(i, top, part):
        at = pl.ds(pl.multiple_of(i * QT, QT), QT)
        total[:, at] = part
        tops[:, at] = jnp.broadcast_to(top, (8, QT))

    run_tiles(heads * rows // QT, keys, kx, vt, qx, sa, sb, rows, None, put)


def fresh_kernel(sizes, parts, scalars, q_ref, own, other, *rest):
    heads, rows, length = sizes
    states = rest[: 2 * parts]
    out, qx, kx, vt, sa, sb = rest[2 * parts :]
    keys = own.shape[0]
    block_rows = keys - rows
    is_key = scalars[0] == 1
    fill_queries(q_ref, qx, heads, rows)
    vt[HD:, :] = jnp.ones((16, keys), BF16)
    kx[:, :HD] = jnp.where(is_key, own[...], other[...])
    vt[:HD, :] = jnp.where(is_key, other[...], own[...]).T
    for b in range(keys // BLK):
        value = 0.0
        if b * BLK < block_rows:
            value = jnp.where(scalars[2 + b] // (length // BLK) >= scalars[1], NEG, 0.0)
        kx[b * BLK : (b + 1) * BLK, HD:] = bias_block(value)

    def put(i, top, part):
        at = pl.ds(pl.multiple_of(i * QT, QT), QT)
        tops = [states[2 * n + 1][0:1, at] for n in range(parts)]
        best = functools.reduce(jnp.maximum, tops, top)
        joined = part * jnp.exp2(top - best)
        for n in range(parts):
            joined = joined + states[2 * n][:, at] * jnp.exp2(tops[n] - best)
        result = joined[:HD] / joined[HD : HD + 1]
        row = lax.rem(i * QT, rows)
        head = lax.div(i * QT, rows)
        out[
            pl.ds(pl.multiple_of(row, QT), QT), pl.ds(pl.multiple_of(head * HD, HD), HD)
        ] = result.T.astype(BF16)

    run_tiles(heads * rows // QT, keys, kx, vt, qx, sa, sb, rows, block_rows, put)


VMEM = pl.BlockSpec(memory_space=pltpu.VMEM)
SMEM = pl.BlockSpec(memory_space=pltpu.SMEM)


def scratch(keys, columns):
    return [
        pltpu.VMEM((2 * HD, columns), BF16),
        pltpu.VMEM((keys, 2 * HD), BF16),
        pltpu.VMEM((HD + 16, keys), BF16),
        pltpu.VMEM((keys, QT), F32),
        pltpu.VMEM((keys, QT), F32),
    ]


def cost(keys, columns):
    return pl.CostEstimate(
        flops=4 * keys * columns * HD, bytes_accessed=4 * keys * HD * 2, transcendentals=keys * columns
    )


def context_part(low, high, sizes, scalars, query_rows, cosine, sine, own, other):
    heads, rows, length = sizes
    keys, columns = (high - low) * length, heads * rows
    return pl.pallas_call(
        functools.partial(context_kernel, low, high, sizes),
        out_shape=(
            jax.ShapeDtypeStruct((HD + 16, columns), F32),
            jax.ShapeDtypeStruct((8, columns), F32),
        ),
        in_specs=[SMEM] + [VMEM] * 5,
        out_specs=(VMEM, VMEM),
        scratch_shapes=scratch(keys, columns),
        compiler_params=pltpu.CompilerParams(vmem_limit_bytes=32 * 2**20),
        cost_estimate=cost(keys, columns),
        name="context_part",
    )(scalars, query_rows, cosine, sine, own, other)


def fresh_part(sizes, scalars, query_rows, own, other, states):
    heads, rows, length = sizes
    keys, columns = own.shape[0], heads * rows
    flat = [array for state in states for array in state]
    return pl.pallas_call(
        functools.partial(fresh_kernel, sizes, len(states)),
        out_shape=jax.ShapeDtypeStruct((rows, heads * HD), BF16),
        in_specs=[SMEM] + [VMEM] * (3 + len(flat)),
        out_specs=VMEM,
        scratch_shapes=scratch(keys, columns),
        compiler_params=pltpu.CompilerParams(vmem_limit_bytes=32 * 2**20),
        cost_estimate=cost(keys, columns),
        name="fresh_part",
    )(scalars, query_rows, own, other, *flat)


def body(
    passage_cache,
    kv_weight,
    block_hidden,
    new_hidden,
    queries,
    passage_ids,
    passage_starts,
    recompute_blocks,
    passage_counts,
):
    req_total = lax.axis_size("req")
    tp_total = lax.axis_size("tp")
    tp_index = lax.axis_index("tp")
    store_dev, length, local_cols = passage_cache.shape
    passages = passage_ids.shape[1]
    piece = length // req_total
    starts = passage_starts[0]
    blocks = recompute_blocks[0]
    is_key = tp_index < tp_total // 2
    scalars = jnp.concatenate(
        [is_key.astype(jnp.int32)[None], passage_counts.astype(jnp.int32), blocks.astype(jnp.int32)]
    )

    outgoing = passage_cache.reshape(store_dev, req_total, piece, local_cols).transpose(1, 0, 2, 3)
    pieces = lax.all_to_all(outgoing, "req", split_axis=0, concat_axis=0, tiled=True)
    pieces = pieces.reshape(req_total * store_dev, piece, local_cols)

    fetched = []
    for low, high in GROUPS:
        ids = passage_ids[:, low:high].reshape(-1)
        send = pick(pieces, ids).reshape(req_total, high - low, piece, local_cols)
        fetched.append(lax.all_to_all(send, "req", split_axis=0, concat_axis=0, tiled=True))
    crossed = [partner(rows, tp_total) for rows in fetched]

    block_rows = block_hidden.shape[1]
    new_count = new_hidden.shape[1]
    local_stack = jnp.concatenate([block_hidden[0], new_hidden[0]], axis=0)
    projected = jnp.dot(
        lax.all_gather(local_stack, "tp", axis=1, tiled=True), kv_weight, preferred_element_type=F32
    )
    block_size = block_rows // blocks.shape[0]
    within = jnp.arange(block_rows, dtype=jnp.int32)
    context_index = blocks[within // block_size] * block_size + within % block_size
    block_positions = starts[context_index // length] + context_index % length
    new_positions = starts[passages] + jnp.arange(new_count, dtype=jnp.int32)
    turned = turn(projected, *tables(jnp.concatenate([block_positions, new_positions])))
    fresh = jnp.where(is_key, turned, projected).astype(BF16)
    fresh_other = partner(fresh, tp_total)

    query_rows = queries[0]
    sizes = (query_rows.shape[1] // HD, new_count, length)
    cosine, sine = tables(starts[:passages])
    states = [
        context_part(low, high, sizes, scalars, query_rows, cosine, sine, own, other)
        for (low, high), own, other in zip(GROUPS, fetched, crossed)
    ]
    return fresh_part(sizes, scalars, query_rows, fresh, fresh_other, states)[None]


def solution(mesh):
    in_specs = (
        P("req", None, "tp"),
        P(None, "tp"),
        P("req", None, "tp"),
        P("req", None, "tp"),
        P("req", None, "tp"),
        P(),
        P("req", None),
        P("req", None),
        P("req"),
    )
    out_specs = P("req", None, "tp")
    return jax.shard_map(body, mesh=mesh, in_specs=in_specs, out_specs=out_specs, check_vma=False)
```

time: 264 us -> 168 us (0.64)
  the two profiles are of different devices: /device:TPU:38 before, /device:TPU:18 now
where the time goes in v1:
time: 168 us; the launch traced here: 167 us
  waiting for transfers between devices  58.6 us (35%)
  starting transfers between devices  44.1 us (26%)
  Pallas kernels  21.8 us (13%)
  between operations  14.3 us (9%)
  other arithmetic  14 us (8%)
  local copies, waits for them, and re-layouts  7.62 us (5%)
  matrix products  6.49 us (4%)
    all_to_all x1, waiting for transfers between devices, body(): lax.all_to_all(outgoing, 'req', split_axis=0, concat_axis=0, tiled=True)  27.8 us
    ppermute x3, waiting for transfers between devices, partner(): lax.ppermute(block, 'tp', [(i, (i + half) % tp_total) for i in range(tp_t...  20.8 us
    ppermute x3, starting transfers between devices, partner(): lax.ppermute(block, 'tp', [(i, (i + half) % tp_total) for i in range(tp_t...  18.6 us
    pallas_call x2, Pallas kernels, context_part(): pl.pallas_call(functools.partial(context_kernel, low, high, sizes), out_s...  15.3 us
    all_to_all x1, starting transfers between devices, body(): lax.all_to_all(outgoing, 'req', split_axis=0, concat_axis=0, tiled=True)  13.6 us
    all_to_all x2, starting transfers between devices, body(): lax.all_to_all(send, 'req', split_axis=0, concat_axis=0, tiled=True)  11.9 us
    all_to_all x2, waiting for transfers between devices, body(): lax.all_to_all(send, 'req', split_axis=0, concat_axis=0, tiled=True)  9.98 us
    gather x2, other arithmetic, body(): block_positions = starts[context_index // length] + context_index % length  6.72 us
  transfers between devices with their start and end apart: 7, of which 4 were waited for; matrix products, arithmetic and copies ran while one was open for 13% of the time, Pallas kernels for 10%

profile of v1, /device:TPU:18, one launch (start us, length us, event | category | flops | bytes accessed | tf_op | source)
XLA Modules:
  0.0 167.0 jit_solution(7933146226571546678)
XLA Ops:
  6.5 2.2 %pad_maximum_fusion = bf16[768,512]{1,0:T(8,128)(2,1)} fusion(bf16[512,512]{1,0:T(8,128)(2,1)} %bitcast.39, bf16[256,512]{1,0:T(8,128)(2,1)} %bitcast.40), kind=kLoop, calls=%fused_computation.1 | loop fusion | flops 1572864 | bytes 1572864 | tf_op jit(solution)/shard_map/concatenate | solution.py:272
  8.8 1.3 copy.26
  10.1 13.6 %all-to-all-start = ((bf16[32,8,16,128]{3,2,1,0:T(8,128)(2,1)}), bf16[32,8,16,128]{3,2,1,0:T(8,128)(2,1)S(1)}, u32[]{:S(2)}, u32[]{:S(2)}) async-start(bf16[32,8,16,128]{3,2,1,0:T(8,128)(2,1)} %bitcast.37), calls=%async_computation | async-start | bytes 2097152 | tf_op jit(solution)/shard_map/all_to_all | solution.py:260
  23.9 27.8 %all-to-all-done = bf16[32,8,16,128]{3,2,1,0:T(8,128)(2,1)S(1)} async-done(((bf16[32,8,16,128]{3,2,1,0:T(8,128)(2,1)}), bf16[32,8,16,128]{3,2,1,0:T(8,128)(2,1)S(1)}, u32[]{:S(2)}, u32[]{:S(2)}) %all-to-all-start) | async-done | bytes 1048608 | tf_op jit(solution)/shard_map/all_to_all | solution.py:260
  52.5 0.8 copy-done.1
  53.2 5.6 %all-to-all-start.1 = ((bf16[32,4,16,128]{3,2,1,0:T(8,128)(2,1)}), bf16[32,4,16,128]{3,2,1,0:T(8,128)(2,1)}, u32[]{:S(2)}, u32[]{:S(2)}) async-start(bf16[32,4,16,128]{3,2,1,0:T(8,128)(2,1)} %bitcast.32), calls=%async_computation.1 | async-start | bytes 1048576 | tf_op jit(solution)/shard_map/all_to_all | solution.py:267
  60.3 1.3 compare_reduce_fusion
  63.0 5.4 %compare_select_fusion.2 = (s32[256,1]{0,1:T(1,128)S(1)}, s32[256,1]{0,1:T(1,128)S(1)}) fusion(s32[]{:T(128)} %bitcast.9, s32[]{:T(128)} %bitcast.10, s32[]{:T(128)} %bitcast.11, s32[]{:T(128)} %bitcast.12, s32[]{:T(128)} %bitcast.13, s32[]{:T(128)} %bitcast.15, s32[]{:T(128)} %bitcast.14, s32[]{:T(128)} %bitcast.6, s32[]{:T(128)} %bitcast.5), kind=kLoop, calls=%fused_computation.19 | loop fusion | flops 12544 | bytes 2084 | tf_op jit(solution)/shard_map/gather | solution.py:279
  68.4 1.2 fusion.6
  71.1 3.6 %all-to-all-done.1.own = bf16[32,4,16,128]{3,2,1,0:T(8,128)(2,1)} async-done(((bf16[32,4,16,128]{3,2,1,0:T(8,128)(2,1)}), bf16[32,4,16,128]{3,2,1,0:T(8,128)(2,1)}, u32[]{:S(2)}, u32[]{:S(2)}) %all-to-all-start.1) | async-done | bytes 524320 | tf_op jit(solution)/shard_map/all_to_all | solution.py:267
  74.7 6.3 %all-to-all-start.2 = ((bf16[32,4,16,128]{3,2,1,0:T(8,128)(2,1)}), bf16[32,4,16,128]{3,2,1,0:T(8,128)(2,1)}, u32[]{:S(2)}, u32[]{:S(2)}) async-start(bf16[32,4,16,128]{3,2,1,0:T(8,128)(2,1)} %bitcast.33), calls=%async_computation.2 | async-start | bytes 1048576 | tf_op jit(solution)/shard_map/all_to_all | solution.py:267
  81.1 5.9 %collective-permute-start.1 = (bf16[32,4,16,128]{3,2,1,0:T(8,128)(2,1)}, bf16[32,4,16,128]{3,2,1,0:T(8,128)(2,1)S(1)}, u32[]{:S(2)}, u32[]{:S(2)}) collective-permute-start(bf16[32,4,16,128]{3,2,1,0:T(8,128)(2,1)} %all-to-all-done.1.own), channel_id=1, source_target_pairs={{0,8},{1,9},{2,10},{3,11},{4,12},{5,13},{6,14},{7,15},{8,0},{9,1},... | collective-permute-start | bytes 1572872 | tf_op jit(solution)/shard_map/ppermute | solution.py:38
  87.2 2.6 %fusion.3 = (f32[768,64]{1,0:T(8,128)}, f32[768,64]{1,0:T(8,128)}, f32[768,64]{1,0:T(8,128)}) fusion(f32[64]{0:T(128)S(1)} %negate_power_fusion, f32[768]{0:T(1024)S(1)} %add_convert_fusion), kind=kLoop, calls=%fused_computation.9 | loop fusion | flops 98304 | bytes 593152 | tf_op jit(solution)/shard_map/neg | solution.py:27
  89.8 6.4 %all-to-all-done.2.own = bf16[32,4,16,128]{3,2,1,0:T(8,128)(2,1)} async-done(((bf16[32,4,16,128]{3,2,1,0:T(8,128)(2,1)}), bf16[32,4,16,128]{3,2,1,0:T(8,128)(2,1)}, u32[]{:S(2)}, u32[]{:S(2)}) %all-to-all-start.2) | async-done | bytes 524320 | tf_op jit(solution)/shard_map/all_to_all | solution.py:267
  96.2 5.9 %collective-permute-start.2 = (bf16[32,4,16,128]{3,2,1,0:T(8,128)(2,1)}, bf16[32,4,16,128]{3,2,1,0:T(8,128)(2,1)}, u32[]{:S(2)}, u32[]{:S(2)}) collective-permute-start(bf16[32,4,16,128]{3,2,1,0:T(8,128)(2,1)} %all-to-all-done.2.own), channel_id=1, source_target_pairs={{0,8},{1,9},{2,10},{3,11},{4,12},{5,13},{6,14},{7,15},{8,0},{9,1},... | collective-permute-start | bytes 1572872 | tf_op jit(solution)/shard_map/ppermute | solution.py:38
  102.2 20.8 %collective-permute-done.1.other = bf16[32,4,16,128]{3,2,1,0:T(8,128)(2,1)S(1)} collective-permute-done((bf16[32,4,16,128]{3,2,1,0:T(8,128)(2,1)}, bf16[32,4,16,128]{3,2,1,0:T(8,128)(2,1)S(1)}, u32[]{:S(2)}, u32[]{:S(2)}) %collective-permute-start.1) | collective-permute-done | bytes 524320 | tf_op jit(solution)/shard_map/ppermute | solution.py:38
  122.9 0.8 copy-done.5
  123.7 1.0 copy-done.3
  124.8 1.0 copy-done.6
  125.8 7.5 %context_part.2 = (f32[144,2048]{1,0:T(8,128)S(1)}, f32[8,2048]{1,0:T(8,128)S(1)}) custom-call(s32[4]{0:T(128)S(1)} %pad_add_fusion.scalars, bf16[512,512]{1,0:T(8,128)(2,1)S(1)} %bitcast.34, f32[8,128]{1,0:T(8,128)S(1)} %get-tuple-element.38.cos_ref, f32[8,128]{1,0:T(8,128)S(1)} %get-tuple-element.39.sin_ref, bf16[32,4,16,128]{3,2,1,0:T(8,128)(2,1)} %all-to-all-done.1.own, ...), custom_call_target="tpu_custom_call" | custom-call | flops 2147483648 | bytes 2097152 | tf_op jit(solution)/shard_map/context_part/pallas_call | solution.py:204
  133.4 6.5 %fusion.14 = f32[768,128]{1,0:T(8,128)S(1)} fusion(bf16[768,8192]{1,0:T(8,128)(2,1)} %all-gather.2.cloned.1.call-done, bf16[8192,128]{1,0:T(8,128)(2,1)S(1)} %copy-done), kind=kOutput, calls=%fused_computation.53 | convolution fusion | flops 1610612736 | bytes 15073280 | tf_op jit(solution)/shard_map/dot_general | solution.py:273
  140.5 6.7 %collective-permute-start = (bf16[768,128]{1,0:T(8,128)(2,1)S(1)}, bf16[768,128]{1,0:T(8,128)(2,1)S(1)}, u32[]{:S(2)}, u32[]{:S(2)}) collective-permute-start(bf16[768,128]{1,0:T(8,128)(2,1)S(1)} %fusion.2.own), channel_id=1, source_target_pairs={{0,8},{1,9},{2,10},{3,11},{4,12},{5,13},{6,14},{7,15},{8,0},{9,1},... | collective-permute-start | bytes 589832 | tf_op jit(solution)/shard_map/ppermute | solution.py:38
  147.3 7.7 %context_part.3 = (f32[144,2048]{1,0:T(8,128)S(1)}, f32[8,2048]{1,0:T(8,128)S(1)}) custom-call(s32[4]{0:T(128)S(1)} %pad_add_fusion.scalars, bf16[512,512]{1,0:T(8,128)(2,1)S(1)} %bitcast.35, f32[8,128]{1,0:T(8,128)S(1)} %get-tuple-element.38.cos_ref, f32[8,128]{1,0:T(8,128)S(1)} %get-tuple-element.39.sin_ref, bf16[32,4,16,128]{3,2,1,0:T(8,128)(2,1)} %all-to-all-done.2.own, ...), custom_call_target="tpu_custom_call" | custom-call | flops 2147483648 | bytes 2097152 | tf_op jit(solution)/shard_map/context_part/pallas_call | solution.py:204
  155.0 5.1 %fresh_part.1 = bf16[512,512]{1,0:T(8,128)(2,1)} custom-call(s32[4]{0:T(128)S(1)} %pad_add_fusion.scalars, bf16[512,512]{1,0:T(8,128)(2,1)S(1)} %bitcast.36, bf16[768,128]{1,0:T(8,128)(2,1)S(1)} %fusion.2.own, bf16[768,128]{1,0:T(8,128)(2,1)S(1)} %collective-permute-done.other, f32[144,2048]{1,0:T(8,128)S(1)} %get-tuple-element.9.rest_0_, ...), custom_call_target="tpu_custom_call" | custom-call | flops 805306368 | bytes 786432 | tf_op jit(solution)/shard_map/fresh_part/pallas_call | solution.py:223
  (47 shorter events, 5.4 us)
Async XLA Ops:
  6.5 126.9 %copy-start = (bf16[8192,128]{1,0:T(8,128)(2,1)S(1)}, bf16[8192,128]{1,0:T(8,128)(2,1)}, u32[]{:S(2)}) copy-start(bf16[8192,128]{1,0:T(8,128)(2,1)} %param.10) | copy-start | bytes 6291460
  6.5 2.2 %copy-start.10 = (bf16[8,512,128]{2,1,0:T(8,128)(2,1)S(1)}, bf16[8,512,128]{2,1,0:T(8,128)(2,1)}, u32[]{:S(2)}) copy-start(bf16[8,512,128]{2,1,0:T(8,128)(2,1)} %param.9) | copy-start | bytes 3145732
  6.5 126.8 %all-gather.2.cloned.1.call-start = ((), (), s32[]{:S(2)}) async-start(), calls=%async_computation.3 | async-start | bytes 13369344 | tf_op jit(solution)/shard_map/all_gather | solution.py:274
  8.8 14.9 %copy-start.13 = (s32[32,8]{0,1:T(8,128)S(1)}, s32[32,8]{0,1:T(8,128)}, u32[]{:S(2)}) copy-start(s32[32,8]{0,1:T(8,128)} %param.14) | copy-start | bytes 3076
  10.1 49.7 %copy-start.12 = (s32[1,2]{1,0:T(1,128)S(1)}, s32[1,2]{1,0:T(1,128)}, u32[]{:S(2)}) copy-start(s32[1,2]{1,0:T(1,128)} %param.16) | copy-start | bytes 28
  10.1 51.6 %copy-start.11 = (s32[1,9]{1,0:T(1,128)S(1)}, s32[1,9]{1,0:T(1,128)}, u32[]{:S(2)}) copy-start(s32[1,9]{1,0:T(1,128)} %param.15) | copy-start | bytes 112
  10.1 41.7 %all-to-all-start = ((bf16[32,8,16,128]{3,2,1,0:T(8,128)(2,1)}), bf16[32,8,16,128]{3,2,1,0:T(8,128)(2,1)S(1)}, u32[]{:S(2)}, u32[]{:S(2)}) async-start(bf16[32,8,16,128]{3,2,1,0:T(8,128)(2,1)} %bitcast.37), calls=%async_computation | async-start | bytes 2097152 | tf_op jit(solution)/shard_map/all_to_all | solution.py:260
  52.5 0.8 copy-start.1
  53.2 21.4 %all-to-all-start.1 = ((bf16[32,4,16,128]{3,2,1,0:T(8,128)(2,1)}), bf16[32,4,16,128]{3,2,1,0:T(8,128)(2,1)}, u32[]{:S(2)}, u32[]{:S(2)}) async-start(bf16[32,4,16,128]{3,2,1,0:T(8,128)(2,1)} %bitcast.32), calls=%async_computation.1 | async-start | bytes 1048576 | tf_op jit(solution)/shard_map/all_to_all | solution.py:267
  70.3 0.8 copy-start.2
  74.7 21.5 %all-to-all-start.2 = ((bf16[32,4,16,128]{3,2,1,0:T(8,128)(2,1)}), bf16[32,4,16,128]{3,2,1,0:T(8,128)(2,1)}, u32[]{:S(2)}, u32[]{:S(2)}) async-start(bf16[32,4,16,128]{3,2,1,0:T(8,128)(2,1)} %bitcast.33), calls=%async_computation.2 | async-start | bytes 1048576 | tf_op jit(solution)/shard_map/all_to_all | solution.py:267
  81.1 41.8 %collective-permute-start.1 = (bf16[32,4,16,128]{3,2,1,0:T(8,128)(2,1)}, bf16[32,4,16,128]{3,2,1,0:T(8,128)(2,1)S(1)}, u32[]{:S(2)}, u32[]{:S(2)}) collective-permute-start(bf16[32,4,16,128]{3,2,1,0:T(8,128)(2,1)} %all-to-all-done.1.own), channel_id=1, source_target_pairs={{0,8},{1,9},{2,10},{3,11},{4,12},{5,13},{6,14},{7,15},{8,0},{9,1},... | collective-permute-start | bytes 1572872 | tf_op jit(solution)/shard_map/ppermute | solution.py:38
  96.2 51.1 %collective-permute-start.2 = (bf16[32,4,16,128]{3,2,1,0:T(8,128)(2,1)}, bf16[32,4,16,128]{3,2,1,0:T(8,128)(2,1)}, u32[]{:S(2)}, u32[]{:S(2)}) collective-permute-start(bf16[32,4,16,128]{3,2,1,0:T(8,128)(2,1)} %all-to-all-done.2.own), channel_id=1, source_target_pairs={{0,8},{1,9},{2,10},{3,11},{4,12},{5,13},{6,14},{7,15},{8,0},{9,1},... | collective-permute-start | bytes 1572872 | tf_op jit(solution)/shard_map/ppermute | solution.py:38
  122.9 0.8 copy-start.5
  123.7 1.0 copy-start.3
  124.8 1.0 copy-start.6
  133.4 6.7 %copy-start.7 = (f32[768,64]{1,0:T(8,128)S(1)}, f32[768,64]{1,0:T(8,128)}, u32[]{:S(2)}) copy-start(f32[768,64]{1,0:T(8,128)} %get-tuple-element.15) | copy-start | bytes 589828
  133.4 6.7 %copy-start.8 = (f32[768,64]{1,0:T(8,128)S(1)}, f32[768,64]{1,0:T(8,128)}, u32[]{:S(2)}) copy-start(f32[768,64]{1,0:T(8,128)} %get-tuple-element.16) | copy-start | bytes 589828
  133.4 6.7 %copy-start.9 = (f32[768,64]{1,0:T(8,128)S(1)}, f32[768,64]{1,0:T(8,128)}, u32[]{:S(2)}) copy-start(f32[768,64]{1,0:T(8,128)} %get-tuple-element.17) | copy-start | bytes 589828
  139.9 7.4 %copy-start.4 = (bf16[1,512,512]{2,1,0:T(8,128)(2,1)S(1)}, bf16[1,512,512]{2,1,0:T(8,128)(2,1)}, u32[]{:S(2)}) copy-start(bf16[1,512,512]{2,1,0:T(8,128)(2,1)} %param.13) | copy-start | bytes 1572868
  140.5 14.5 %collective-permute-start = (bf16[768,128]{1,0:T(8,128)(2,1)S(1)}, bf16[768,128]{1,0:T(8,128)(2,1)S(1)}, u32[]{:S(2)}, u32[]{:S(2)}) collective-permute-start(bf16[768,128]{1,0:T(8,128)(2,1)S(1)} %fusion.2.own), channel_id=1, source_target_pairs={{0,8},{1,9},{2,10},{3,11},{4,12},{5,13},{6,14},{7,15},{8,0},{9,1},... | collective-permute-start | bytes 589832 | tf_op jit(solution)/shard_map/ppermute | solution.py:38
Sparse Core Ops, SparseCore 0:
  9.5 85.3 all-gather.1

commit v2 on v1

--- a/solution.py
+++ b/solution.py
@@ -115,7 +115,8 @@
     lax.fori_loop(0, tiles // 2, step, top)
 
 
-def context_kernel(low, high, sizes, scalars, q_ref, cos_ref, sin_ref, own, other, total, tops, qx, kx, vt, sa, sb):
+def context_kernel(low, high, sizes, scalars, q_ref, cos_ref, sin_ref, own, other, *rest):
+    total, tops, qx, kx, vt, sa, sb = rest[-7:]
     heads, rows, length = sizes
     keys = (high - low) * length
     is_key = scalars[0] == 1
@@ -198,7 +199,7 @@
     )
 
 
-def context_part(low, high, sizes, scalars, query_rows, cosine, sine, own, other):
+def context_part(low, high, sizes, scalars, query_rows, cosine, sine, own, other, after):
     heads, rows, length = sizes
     keys, columns = (high - low) * length, heads * rows
     return pl.pallas_call(
@@ -207,13 +208,13 @@
             jax.ShapeDtypeStruct((HD + 16, columns), F32),
             jax.ShapeDtypeStruct((8, columns), F32),
         ),
-        in_specs=[SMEM] + [VMEM] * 5,
+        in_specs=[SMEM] + [VMEM] * 5 + [pl.BlockSpec(memory_space=pl.ANY)] * len(after),
         out_specs=(VMEM, VMEM),
         scratch_shapes=scratch(keys, columns),
         compiler_params=pltpu.CompilerParams(vmem_limit_bytes=32 * 2**20),
         cost_estimate=cost(keys, columns),
         name="context_part",
-    )(scalars, query_rows, cosine, sine, own, other)
+    )(scalars, query_rows, cosine, sine, own, other, *after)
 
 
 def fresh_part(sizes, scalars, query_rows, own, other, states):
@@ -286,7 +287,7 @@
     sizes = (query_rows.shape[1] // HD, new_count, length)
     cosine, sine = tables(starts[:passages])
     states = [
-        context_part(low, high, sizes, scalars, query_rows, cosine, sine, own, other)
+        context_part(low, high, sizes, scalars, query_rows, cosine, sine, own, other, (fresh,))
         for (low, high), own, other in zip(GROUPS, fetched, crossed)
     ]
     return fresh_part(sizes, scalars, query_rows, fresh, fresh_other, states)[None]

time: 168 us -> 163 us (0.970)
  the two profiles are of different devices: /device:TPU:18 before, /device:TPU:2 now
where the time goes in v2:
time: 163 us; the launch traced here: 162 us
  waiting for transfers between devices  58.7 us (36%)
  starting transfers between devices  42.9 us (26%)
  Pallas kernels  21.3 us (13%)
  between operations  14.3 us (9%)
  other arithmetic  13.7 us (8%)
  matrix products  6.47 us (4%)
  local copies, waits for them, and re-layouts  4.83 us (3%)
    all_to_all x1, waiting for transfers between devices, body(): lax.all_to_all(outgoing, 'req', split_axis=0, concat_axis=0, tiled=True)  27.8 us
    ppermute x3, waiting for transfers between devices, partner(): lax.ppermute(block, 'tp', [(i, (i + half) % tp_total) for i in range(tp_t...  22.4 us
    ppermute x3, starting transfers between devices, partner(): lax.ppermute(block, 'tp', [(i, (i + half) % tp_total) for i in range(tp_t...  17.5 us
    pallas_call x2, Pallas kernels, context_part(): pl.pallas_call(functools.partial(context_kernel, low, high, sizes), out_s...  14.8 us
    all_to_all x1, starting transfers between devices, body(): lax.all_to_all(outgoing, 'req', split_axis=0, concat_axis=0, tiled=True)  13.6 us
    all_to_all x2, starting transfers between devices, body(): lax.all_to_all(send, 'req', split_axis=0, concat_axis=0, tiled=True)  11.7 us
    all_to_all x2, waiting for transfers between devices, body(): lax.all_to_all(send, 'req', split_axis=0, concat_axis=0, tiled=True)  8.37 us
    gather x2, other arithmetic, body(): block_positions = starts[context_index // length] + context_index % length  6.51 us
  transfers between devices with their start and end apart: 7, of which 5 were waited for; matrix products, arithmetic and copies ran while one was open for 13% of the time, Pallas kernels for 10%

profile of v2, /device:TPU:2, one launch (start us, length us, event | category | flops | bytes accessed | tf_op | source)
XLA Modules:
  0.0 162.2 jit_solution(7364705669238699240)
XLA Ops:
  6.5 2.2 %pad_maximum_fusion = bf16[768,512]{1,0:T(8,128)(2,1)} fusion(bf16[512,512]{1,0:T(8,128)(2,1)} %bitcast.39, bf16[256,512]{1,0:T(8,128)(2,1)} %bitcast.40), kind=kLoop, calls=%fused_computation.1 | loop fusion | flops 1572864 | bytes 1572864 | tf_op jit(solution)/shard_map/concatenate | solution.py:273
  8.8 1.3 copy.26
  10.1 13.6 %all-to-all-start = ((bf16[32,8,16,128]{3,2,1,0:T(8,128)(2,1)}), bf16[32,8,16,128]{3,2,1,0:T(8,128)(2,1)S(1)}, u32[]{:S(2)}, u32[]{:S(2)}) async-start(bf16[32,8,16,128]{3,2,1,0:T(8,128)(2,1)} %bitcast.37), calls=%async_computation | async-start | bytes 2097152 | tf_op jit(solution)/shard_map/all_to_all | solution.py:261
  23.9 27.8 %all-to-all-done = bf16[32,8,16,128]{3,2,1,0:T(8,128)(2,1)S(1)} async-done(((bf16[32,8,16,128]{3,2,1,0:T(8,128)(2,1)}), bf16[32,8,16,128]{3,2,1,0:T(8,128)(2,1)S(1)}, u32[]{:S(2)}, u32[]{:S(2)}) %all-to-all-start) | async-done | bytes 1048608 | tf_op jit(solution)/shard_map/all_to_all | solution.py:261
  52.5 0.8 copy-done.1
  53.3 5.6 %all-to-all-start.1 = ((bf16[32,4,16,128]{3,2,1,0:T(8,128)(2,1)}), bf16[32,4,16,128]{3,2,1,0:T(8,128)(2,1)}, u32[]{:S(2)}, u32[]{:S(2)}) async-start(bf16[32,4,16,128]{3,2,1,0:T(8,128)(2,1)} %bitcast.32), calls=%async_computation.1 | async-start | bytes 1048576 | tf_op jit(solution)/shard_map/all_to_all | solution.py:268
  60.4 1.2 compare_reduce_fusion
  63.0 5.3 %compare_select_fusion.2 = (s32[256,1]{0,1:T(1,128)S(1)}, s32[256,1]{0,1:T(1,128)S(1)}) fusion(s32[]{:T(128)} %bitcast.9, s32[]{:T(128)} %bitcast.10, s32[]{:T(128)} %bitcast.11, s32[]{:T(128)} %bitcast.12, s32[]{:T(128)} %bitcast.13, s32[]{:T(128)} %bitcast.15, s32[]{:T(128)} %bitcast.14, s32[]{:T(128)} %bitcast.6, s32[]{:T(128)} %bitcast.5), kind=kLoop, calls=%fused_computation.19 | loop fusion | flops 12544 | bytes 2084 | tf_op jit(solution)/shard_map/gather | solution.py:280
  68.3 1.3 fusion.6
  69.6 0.7 pick.3
  70.3 0.8 copy-done.2
  71.1 3.7 %all-to-all-done.1.own = bf16[32,4,16,128]{3,2,1,0:T(8,128)(2,1)} async-done(((bf16[32,4,16,128]{3,2,1,0:T(8,128)(2,1)}), bf16[32,4,16,128]{3,2,1,0:T(8,128)(2,1)}, u32[]{:S(2)}, u32[]{:S(2)}) %all-to-all-start.1) | async-done | bytes 524320 | tf_op jit(solution)/shard_map/all_to_all | solution.py:268
  74.7 6.1 %all-to-all-start.2 = ((bf16[32,4,16,128]{3,2,1,0:T(8,128)(2,1)}), bf16[32,4,16,128]{3,2,1,0:T(8,128)(2,1)S(1)}, u32[]{:S(2)}, u32[]{:S(2)}) async-start(bf16[32,4,16,128]{3,2,1,0:T(8,128)(2,1)} %bitcast.33), calls=%async_computation.2 | async-start | bytes 1048576 | tf_op jit(solution)/shard_map/all_to_all | solution.py:268
  81.1 2.5 %fusion.3 = (f32[768,64]{1,0:T(8,128)S(1)}, f32[768,64]{1,0:T(8,128)}, f32[768,64]{1,0:T(8,128)}) fusion(f32[64]{0:T(128)S(1)} %negate_power_fusion, f32[768]{0:T(1024)S(1)} %add_convert_fusion), kind=kLoop, calls=%fused_computation.9 | loop fusion | flops 98304 | bytes 593152 | tf_op jit(solution)/shard_map/neg | solution.py:27
  83.6 7.7 %collective-permute-start.1 = (bf16[32,4,16,128]{3,2,1,0:T(8,128)(2,1)}, bf16[32,4,16,128]{3,2,1,0:T(8,128)(2,1)}, u32[]{:S(2)}, u32[]{:S(2)}) collective-permute-start(bf16[32,4,16,128]{3,2,1,0:T(8,128)(2,1)} %all-to-all-done.1.own), channel_id=1, source_target_pairs={{0,8},{1,9},{2,10},{3,11},{4,12},{5,13},{6,14},{7,15},{8,0},{9,1},... | collective-permute-start | bytes 1572872 | tf_op jit(solution)/shard_map/ppermute | solution.py:38
  91.3 4.7 %all-to-all-done.2.own = bf16[32,4,16,128]{3,2,1,0:T(8,128)(2,1)S(1)} async-done(((bf16[32,4,16,128]{3,2,1,0:T(8,128)(2,1)}), bf16[32,4,16,128]{3,2,1,0:T(8,128)(2,1)S(1)}, u32[]{:S(2)}, u32[]{:S(2)}) %all-to-all-start.2) | async-done | bytes 524320 | tf_op jit(solution)/shard_map/all_to_all | solution.py:268
  96.1 7.7 %collective-permute-start.2 = (bf16[32,4,16,128]{3,2,1,0:T(8,128)(2,1)S(1)}, bf16[32,4,16,128]{3,2,1,0:T(8,128)(2,1)S(1)}, u32[]{:S(2)}, u32[]{:S(2)}) collective-permute-start(bf16[32,4,16,128]{3,2,1,0:T(8,128)(2,1)S(1)} %all-to-all-done.2.own), channel_id=1, source_target_pairs={{0,8},{1,9},{2,10},{3,11},{4,12},{5,13},{6,14},{7,15},{8,0},{9,1},... | collective-permute-start | bytes 1572872 | tf_op jit(solution)/shard_map/ppermute | solution.py:38
  103.9 6.5 %fusion.14 = f32[768,128]{1,0:T(8,128)S(1)} fusion(bf16[768,8192]{1,0:T(8,128)(2,1)} %all-gather.2.cloned.1.call-done, bf16[8192,128]{1,0:T(8,128)(2,1)S(1)} %copy-done), kind=kOutput, calls=%fused_computation.53 | convolution fusion | flops 1610612736 | bytes 15073280 | tf_op jit(solution)/shard_map/dot_general | solution.py:274
  110.9 2.1 %collective-permute-start = (bf16[768,128]{1,0:T(8,128)(2,1)S(1)}, bf16[768,128]{1,0:T(8,128)(2,1)S(1)}, u32[]{:S(2)}, u32[]{:S(2)}) collective-permute-start(bf16[768,128]{1,0:T(8,128)(2,1)S(1)} %fusion.2.rest_0_.own), channel_id=1, source_target_pairs={{0,8},{1,9},{2,10},{3,11},{4,12},{5,13},{6,14},{7,15},{8,0},{9,1},... | collective-permute-start | bytes 589832 | tf_op jit(solution)/shard_map/ppermute | solution.py:38
  113.0 16.6 %collective-permute-done.1.other = bf16[32,4,16,128]{3,2,1,0:T(8,128)(2,1)} collective-permute-done((bf16[32,4,16,128]{3,2,1,0:T(8,128)(2,1)}, bf16[32,4,16,128]{3,2,1,0:T(8,128)(2,1)}, u32[]{:S(2)}, u32[]{:S(2)}) %collective-permute-start.1) | collective-permute-done | bytes 524320 | tf_op jit(solution)/shard_map/ppermute | solution.py:38
  129.7 7.7 %context_part.2 = (f32[144,2048]{1,0:T(8,128)S(1)}, f32[8,2048]{1,0:T(8,128)S(1)}) custom-call(s32[4]{0:T(128)S(1)} %pad_add_fusion.scalars, bf16[512,512]{1,0:T(8,128)(2,1)S(1)} %bitcast.34, f32[8,128]{1,0:T(8,128)S(1)} %get-tuple-element.38.cos_ref, f32[8,128]{1,0:T(8,128)S(1)} %get-tuple-element.39.sin_ref, bf16[32,4,16,128]{3,2,1,0:T(8,128)(2,1)} %all-to-all-done.1.own, ...), custom_call_target="tpu_custom_call" | custom-call | flops 2147483648 | bytes 2097152 | tf_op jit(solution)/shard_map/context_part/pallas_call | solution.py:205
  137.4 5.8 %collective-permute-done.2.other = bf16[32,4,16,128]{3,2,1,0:T(8,128)(2,1)S(1)} collective-permute-done((bf16[32,4,16,128]{3,2,1,0:T(8,128)(2,1)S(1)}, bf16[32,4,16,128]{3,2,1,0:T(8,128)(2,1)S(1)}, u32[]{:S(2)}, u32[]{:S(2)}) %collective-permute-start.2) | collective-permute-done | bytes 524320 | tf_op jit(solution)/shard_map/ppermute | solution.py:38
  143.2 7.1 %context_part.3 = (f32[144,2048]{1,0:T(8,128)S(1)}, f32[8,2048]{1,0:T(8,128)S(1)}) custom-call(s32[4]{0:T(128)S(1)} %pad_add_fusion.scalars, bf16[512,512]{1,0:T(8,128)(2,1)S(1)} %bitcast.35, f32[8,128]{1,0:T(8,128)S(1)} %get-tuple-element.38.cos_ref, f32[8,128]{1,0:T(8,128)S(1)} %get-tuple-element.39.sin_ref, ...), custom_call_target="tpu_custom_call" | custom-call | flops 2147483648 | bytes 2097152 | tf_op jit(solution)/shard_map/context_part/pallas_call | solution.py:205
  150.3 5.1 %fresh_part.1 = bf16[512,512]{1,0:T(8,128)(2,1)} custom-call(s32[4]{0:T(128)S(1)} %pad_add_fusion.scalars, bf16[512,512]{1,0:T(8,128)(2,1)S(1)} %bitcast.36, bf16[768,128]{1,0:T(8,128)(2,1)S(1)} %fusion.2.rest_0_.own, bf16[768,128]{1,0:T(8,128)(2,1)S(1)} %collective-permute-done.other, f32[144,2048]{1,0:T(8,128)S(1)} %get-tuple-element.9.rest_0_, ...), custom_call_target="tpu_custom_call" | custom-call | flops 805306368 | bytes 786432 | tf_op jit(solution)/shard_map/fresh_part/pallas_call | solution.py:224
  (39 shorter events, 4.0 us)
Async XLA Ops:
  6.5 97.3 %copy-start = (bf16[8192,128]{1,0:T(8,128)(2,1)S(1)}, bf16[8192,128]{1,0:T(8,128)(2,1)}, u32[]{:S(2)}) copy-start(bf16[8192,128]{1,0:T(8,128)(2,1)} %param.10) | copy-start | bytes 6291460
  6.5 2.2 %copy-start.6 = (bf16[8,512,128]{2,1,0:T(8,128)(2,1)S(1)}, bf16[8,512,128]{2,1,0:T(8,128)(2,1)}, u32[]{:S(2)}) copy-start(bf16[8,512,128]{2,1,0:T(8,128)(2,1)} %param.9) | copy-start | bytes 3145732
  6.5 97.3 %all-gather.2.cloned.1.call-start = ((), (), s32[]{:S(2)}) async-start(), calls=%async_computation.3 | async-start | bytes 13369344 | tf_op jit(solution)/shard_map/all_gather | solution.py:275
  8.8 14.9 %copy-start.9 = (s32[32,8]{0,1:T(8,128)S(1)}, s32[32,8]{0,1:T(8,128)}, u32[]{:S(2)}) copy-start(s32[32,8]{0,1:T(8,128)} %param.14) | copy-start | bytes 3076
  10.1 49.7 %copy-start.8 = (s32[1,2]{1,0:T(1,128)S(1)}, s32[1,2]{1,0:T(1,128)}, u32[]{:S(2)}) copy-start(s32[1,2]{1,0:T(1,128)} %param.16) | copy-start | bytes 28
  10.1 51.5 %copy-start.7 = (s32[1,9]{1,0:T(1,128)S(1)}, s32[1,9]{1,0:T(1,128)}, u32[]{:S(2)}) copy-start(s32[1,9]{1,0:T(1,128)} %param.15) | copy-start | bytes 112
  10.1 41.7 %all-to-all-start = ((bf16[32,8,16,128]{3,2,1,0:T(8,128)(2,1)}), bf16[32,8,16,128]{3,2,1,0:T(8,128)(2,1)S(1)}, u32[]{:S(2)}, u32[]{:S(2)}) async-start(bf16[32,8,16,128]{3,2,1,0:T(8,128)(2,1)} %bitcast.37), calls=%async_computation | async-start | bytes 2097152 | tf_op jit(solution)/shard_map/all_to_all | solution.py:261
  52.5 0.8 copy-start.1
  53.3 21.4 %all-to-all-start.1 = ((bf16[32,4,16,128]{3,2,1,0:T(8,128)(2,1)}), bf16[32,4,16,128]{3,2,1,0:T(8,128)(2,1)}, u32[]{:S(2)}, u32[]{:S(2)}) async-start(bf16[32,4,16,128]{3,2,1,0:T(8,128)(2,1)} %bitcast.32), calls=%async_computation.1 | async-start | bytes 1048576 | tf_op jit(solution)/shard_map/all_to_all | solution.py:268
  70.3 0.8 copy-start.2
  74.7 21.3 %all-to-all-start.2 = ((bf16[32,4,16,128]{3,2,1,0:T(8,128)(2,1)}), bf16[32,4,16,128]{3,2,1,0:T(8,128)(2,1)S(1)}, u32[]{:S(2)}, u32[]{:S(2)}) async-start(bf16[32,4,16,128]{3,2,1,0:T(8,128)(2,1)} %bitcast.33), calls=%async_computation.2 | async-start | bytes 1048576 | tf_op jit(solution)/shard_map/all_to_all | solution.py:268
  83.6 46.0 %collective-permute-start.1 = (bf16[32,4,16,128]{3,2,1,0:T(8,128)(2,1)}, bf16[32,4,16,128]{3,2,1,0:T(8,128)(2,1)}, u32[]{:S(2)}, u32[]{:S(2)}) collective-permute-start(bf16[32,4,16,128]{3,2,1,0:T(8,128)(2,1)} %all-to-all-done.1.own), channel_id=1, source_target_pairs={{0,8},{1,9},{2,10},{3,11},{4,12},{5,13},{6,14},{7,15},{8,0},{9,1},... | collective-permute-start | bytes 1572872 | tf_op jit(solution)/shard_map/ppermute | solution.py:38
  96.1 47.1 %collective-permute-start.2 = (bf16[32,4,16,128]{3,2,1,0:T(8,128)(2,1)S(1)}, bf16[32,4,16,128]{3,2,1,0:T(8,128)(2,1)S(1)}, u32[]{:S(2)}, u32[]{:S(2)}) collective-permute-start(bf16[32,4,16,128]{3,2,1,0:T(8,128)(2,1)S(1)} %all-to-all-done.2.own), channel_id=1, source_target_pairs={{0,8},{1,9},{2,10},{3,11},{4,12},{5,13},{6,14},{7,15},{8,0},{9,1},... | collective-permute-start | bytes 1572872 | tf_op jit(solution)/shard_map/ppermute | solution.py:38
  103.8 6.7 %copy-start.4 = (f32[768,64]{1,0:T(8,128)S(1)}, f32[768,64]{1,0:T(8,128)}, u32[]{:S(2)}) copy-start(f32[768,64]{1,0:T(8,128)} %get-tuple-element.16) | copy-start | bytes 589828
  103.8 6.7 %copy-start.5 = (f32[768,64]{1,0:T(8,128)S(1)}, f32[768,64]{1,0:T(8,128)}, u32[]{:S(2)}) copy-start(f32[768,64]{1,0:T(8,128)} %get-tuple-element.17) | copy-start | bytes 589828
  110.3 19.3 %copy-start.3 = (bf16[1,512,512]{2,1,0:T(8,128)(2,1)S(1)}, bf16[1,512,512]{2,1,0:T(8,128)(2,1)}, u32[]{:S(2)}) copy-start(bf16[1,512,512]{2,1,0:T(8,128)(2,1)} %param.13) | copy-start | bytes 1572868
  110.9 39.3 %collective-permute-start = (bf16[768,128]{1,0:T(8,128)(2,1)S(1)}, bf16[768,128]{1,0:T(8,128)(2,1)S(1)}, u32[]{:S(2)}, u32[]{:S(2)}) collective-permute-start(bf16[768,128]{1,0:T(8,128)(2,1)S(1)} %fusion.2.rest_0_.own), channel_id=1, source_target_pairs={{0,8},{1,9},{2,10},{3,11},{4,12},{5,13},{6,14},{7,15},{8,0},{9,1},... | collective-permute-start | bytes 589832 | tf_op jit(solution)/shard_map/ppermute | solution.py:38
Sparse Core Ops, SparseCore 0:
  9.5 82.9 all-gather.1
